TPU v7x, 256 devices: a whole 4x4x8 slice. The times are simulated.
256 devices in a mesh: ctx: 32 (over x, z), head: 8 (over y, core).
Axes of the slice: x: 4, y: 4, z: 8, core: 2. Of those that a mesh axis runs over, the one named last changes fastest.
Arguments:
- queries: bfloat16 [16384, 4096], P('ctx', 'head'), may hold values from -5 to 5
- key_rows: bfloat16 [16384, 1024], P('ctx', 'head'), may hold values from -5 to 5
- value_rows: bfloat16 [16384, 1024], P('ctx', 'head'), may hold values from -6 to 6
- slash_offsets: int32 [32, 4], P('head'), may hold values from 0 to 8, as said below
- union_blocks: int32 [8, 32, 2], P('head'), may hold values from 0 to 7, as said below
- head_picks: int32 [32, 32, 1], P('head'), may hold values from 0 to 1, as said below
- owner_counts: int32 [32, 32], P('head'), may hold values from 0 to 1, as said below
- out_weight: bfloat16 [4096, 4096], P(None, 'head'), may hold values from -0.09375 to 0.09375
Outputs:
- projected: bfloat16 [16384, 4096], P('ctx', 'head')
Inputs may be any that keep to these rules, and one draw needn't show every extreme that they name: `slash_offsets`: each head's offsets are distinct and include 0 and 8. `union_blocks`: the 2 entries of each KV head and sequence block are distinct. `head_picks`: the 1 entries of each query head and sequence block are distinct. `owner_counts`: equal to 1 for sequence block 0.
All inputs are finite; a program needn't handle non-finite values.
Results may differ from a plain program's by a relative error of at most 0.0056.
Values may be sent and summed in bfloat16 or wider, within the bound.
A program may use at most 128 MiB of HBM per device.

v0:
```python
import jax
import jax.numpy as jnp
from jax import lax
from jax.sharding import PartitionSpec as P

HEAD_SIZE = 128
BLOCK_TOKENS = 64
NS = 4
VPER = 1


def from_behind(array, axis, by):
    length = lax.axis_size(axis)
    pairs = [(i, i + by) for i in range(length) if 0 <= i + by < length]
    return lax.ppermute(array, axis, pairs)


def attend(
    vert_scores, vert_mask, diagonal_scores, slash_mask, vert_values, diagonal_values, per_dev
):
    masked_vert = jnp.where(vert_mask, vert_scores, -1e30)
    masked_slash = jnp.where(slash_mask, diagonal_scores, -1e30)
    peak = jnp.maximum(
        jnp.max(masked_vert, axis=-1, keepdims=True), jnp.max(masked_slash, axis=-1, keepdims=True)
    )
    weight_vert = jnp.exp(masked_vert - peak)
    weight_slash = jnp.exp(masked_slash - peak)
    total = jnp.sum(weight_vert, axis=-1, keepdims=True) + jnp.sum(
        weight_slash, axis=-1, keepdims=True
    )
    prob_vert = weight_vert.astype(jnp.bfloat16)
    slash_probability = weight_slash.astype(jnp.bfloat16).reshape(
        per_dev, BLOCK_TOKENS, NS, BLOCK_TOKENS
    )
    numer = jnp.dot(prob_vert, vert_values, preferred_element_type=jnp.float32)
    diagonal_portion = jnp.einsum(
        "wojf,wjfl->wol", slash_probability, diagonal_values, preferred_element_type=jnp.float32
    )
    numer = numer + diagonal_portion.reshape(per_dev * BLOCK_TOKENS, HEAD_SIZE)
    return (numer / total).astype(jnp.bfloat16)


def shards(
    queries, key_rows, value_rows, slash_offsets, union_blocks, head_picks, owner_counts, out_weight
):
    tokens = queries.shape[0]
    per_dev = tokens // BLOCK_TOKENS
    heads_here = slash_offsets.shape[0]
    groups_here = key_rows.shape[1] // HEAD_SIZE
    group_size = heads_here // groups_here
    owners = lax.axis_size("ctx")
    device_rank = lax.axis_index("ctx")
    scale_of_scores = jnp.float32(HEAD_SIZE ** (-0.5))
    stacked = jnp.stack([key_rows, value_rows])
    previous = from_behind(stacked, "ctx", 1)
    extended = jnp.concatenate([previous, stacked], axis=1).reshape(
        2, 2 * per_dev, BLOCK_TOKENS, groups_here, HEAD_SIZE
    )
    local_blocks = stacked.reshape(2, per_dev, BLOCK_TOKENS, groups_here, HEAD_SIZE)
    head_group = jnp.arange(heads_here, dtype=jnp.int32) // group_size
    mine_union = lax.dynamic_index_in_dim(union_blocks, device_rank, 1, keepdims=False)
    owner_base = jnp.arange(owners, dtype=jnp.int32)[:, None] * per_dev
    slot_rank = jnp.arange(VPER, dtype=jnp.int32)
    chosen = slot_rank[None, None, :] < owner_counts[:, :, None]
    mine_picks = lax.dynamic_index_in_dim(head_picks, device_rank, 1, keepdims=False)
    chosen_local = jnp.take_along_axis(mine_union[head_group], mine_picks, axis=1)
    block_rows = local_blocks[:, chosen_local, :, head_group[:, None], :]
    gathered = lax.all_gather(block_rows[:, None], "ctx", axis=1, tiled=True)
    slot_block = owner_base[None] + jnp.take_along_axis(
        union_blocks[head_group], head_picks, axis=2
    )
    source_of = list(range(heads_here))
    query_place = device_rank * tokens + jnp.arange(tokens, dtype=jnp.int32)
    query_block = device_rank * per_dev + jnp.arange(per_dev, dtype=jnp.int32)
    inner_offset = jnp.arange(BLOCK_TOKENS, dtype=jnp.int32)
    local_index = jnp.arange(per_dev, dtype=jnp.int32)
    per_head = []
    for head_index in range(heads_here):
        kv_index = head_index // group_size
        offsets = slash_offsets[head_index]
        query_head = queries[:, head_index * HEAD_SIZE : (head_index + 1) * HEAD_SIZE]
        vertical = gathered[source_of[head_index]]
        blocks_flat = slot_block[head_index].reshape(-1)
        valid_flat = chosen[head_index].reshape(-1)
        slot_count = blocks_flat.shape[0]
        vert_keys = vertical[:, :, 0].reshape(slot_count * BLOCK_TOKENS, HEAD_SIZE)
        vert_values = vertical[:, :, 1].reshape(slot_count * BLOCK_TOKENS, HEAD_SIZE)
        vert_scores = (
            jnp.einsum("qd,kd->qk", query_head, vert_keys, preferred_element_type=jnp.float32)
            * scale_of_scores
        )
        distance = query_block[:, None] - blocks_flat[None, :]
        on_slash = jnp.any(distance[:, :, None] == offsets[None, None, :], axis=2)
        block_mask = valid_flat[None, :] & jnp.logical_not(on_slash)
        key_place = (blocks_flat[:, None] * BLOCK_TOKENS + inner_offset[None, :]).reshape(-1)
        vert_mask = jnp.broadcast_to(
            block_mask[:, None, :, None], (per_dev, BLOCK_TOKENS, slot_count, BLOCK_TOKENS)
        ).reshape(tokens, slot_count * BLOCK_TOKENS)
        vert_mask = vert_mask & (key_place[None, :] <= query_place[:, None])
        group_slab = extended[:, :, :, kv_index, :]
        ext_index = local_index[:, None] + per_dev - offsets[None, :]
        slash_rows = group_slab[:, ext_index]
        diagonal_scores = (
            jnp.einsum(
                "hax,hisx->hais",
                query_head.reshape(per_dev, BLOCK_TOKENS, HEAD_SIZE),
                slash_rows[0],
                preferred_element_type=jnp.float32,
            )
            * scale_of_scores
        )
        slash_valid = query_block[:, None] - offsets[None, :] >= 0
        slash_mask = slash_valid[:, None, :, None] & (
            (offsets[None, None, :, None] > 0)
            | (inner_offset[None, None, None, :] <= inner_offset[None, :, None, None])
        )
        slash_mask = slash_mask.reshape(tokens, NS * BLOCK_TOKENS)
        per_head.append(
            attend(
                vert_scores,
                vert_mask,
                diagonal_scores.reshape(tokens, NS * BLOCK_TOKENS),
                slash_mask,
                vert_values,
                slash_rows[1],
                per_dev,
            )
        )
    attended = jnp.concatenate(per_head, axis=1)
    projected = jnp.dot(
        lax.all_gather(attended, "head", axis=1, tiled=True),
        out_weight,
        preferred_element_type=jnp.float32,
    )
    return projected.astype(jnp.bfloat16)


def solution(mesh):
    in_specs = (
        P("ctx", "head"),
        P("ctx", "head"),
        P("ctx", "head"),
        P("head", None),
        P("head", None, None),
        P("head", None, None),
        P("head", None),
        P(None, "head"),
    )
    out_specs = P("ctx", "head")
    return jax.shard_map(shards, mesh=mesh, in_specs=in_specs, out_specs=out_specs, check_vma=False)
```

profile of v0, /device:TPU:1, one launch (start us, length us, event | category | flops | bytes accessed | tf_op | source)
XLA Modules:
  0.0 189.1 jit_solution(1846127941252690670)
XLA Ops:
  12.4 4.4 %collective-permute-start = (bf16[2,512,128]{2,1,0:T(8,128)(2,1)S(1)}, bf16[2,512,128]{2,1,0:T(8,128)(2,1)S(1)}, u32[]{:S(2)}, u32[]{:S(2)}) collective-permute-start(bf16[2,512,128]{2,1,0:T(8,128)(2,1)S(1)} %pad_maximum_fusion.2), channel_id=1, source_target_pairs={{0,8},{8,16},{16,24},{24,32},{32,40},{40,48},{48,56},{56,64},{64,7... | collective-permute-start | bytes 786440 | tf_op jit(solution)/shard_map/ppermute | solution.py:15
  18.3 1.5 gather_fusion.5
  23.7 4.7 %reshape.1051 = pred[512,2048]{0,1:T(32,128)(4,1)} reshape(pred[8,64,32,64]{1,0,3,2:T(8,128)(4,1)S(1)} %broadcast_in_dim.29) | data formatting | bytes 2097152 | tf_op jit(solution)/shard_map/reshape | solution.py:98
  29.8 4.7 %reshape.1054 = pred[512,2048]{0,1:T(32,128)(4,1)} reshape(pred[8,64,32,64]{1,0,3,2:T(8,128)(4,1)S(1)} %broadcast_in_dim.33) | data formatting | bytes 2097152 | tf_op jit(solution)/shard_map/reshape | solution.py:98
  35.9 4.7 %reshape.1057 = pred[512,2048]{0,1:T(32,128)(4,1)} reshape(pred[8,64,32,64]{1,0,3,2:T(8,128)(4,1)S(1)} %broadcast_in_dim.34) | data formatting | bytes 2097152 | tf_op jit(solution)/shard_map/reshape | solution.py:98
  42.0 4.7 %reshape.1060 = pred[512,2048]{0,1:T(32,128)(4,1)} reshape(pred[8,64,32,64]{1,0,3,2:T(8,128)(4,1)S(1)} %broadcast_in_dim.35) | data formatting | bytes 2097152 | tf_op jit(solution)/shard_map/reshape | solution.py:98
  50.0 1.3 fusion.107
  57.2 1.7 gather_fusion.4
  58.9 1.3 copy.70
  61.6 32.7 %all-gather.6.cloned.1.call-done = bf16[4,64,64,128]{3,2,1,0:T(8,128)(2,1)} async-done(((bf16[4,2,64,128]{3,2,1,0:T(8,128)(2,1)}), bf16[4,64,64,128]{3,2,1,0:T(8,128)(2,1)}) %all-gather.6.cloned.1.call-update) | async-done | bytes 4194320 | tf_op jit(solution)/shard_map/all_gather | solution.py:68
  94.4 4.4 %fusion.94 = (bf16[1,64,64,128]{3,2,1,0:T(8,128)(2,1)S(1)}, bf16[1,64,64,128]{3,2,1,0:T(8,128)(2,1)}, bf16[1,64,64,128]{3,2,1,0:T(8,128)(2,1)}, bf16[1,64,64,128]{3,2,1,0:T(8,128)(2,1)}) fusion(bf16[4,64,64,128]{3,2,1,0:T(8,128)(2,1)} %all-gather.6.cloned.1.call-done), kind=kLoop, calls=%fused_computation.176 | loop fusion | bytes 8388608 | tf_op jit(solution)/shard_map/slice | solution.py:82
  99.6 3.6 %fusion.106 = (f32[512]{0:T(512)S(1)}, f32[512,2048]{0,1:T(8,128)}) fusion(bf16[2048,128]{1,0:T(8,128)(2,1)S(1)} %bitcast.252, bf16[512,512]{1,0:T(8,128)(2,1)} %param.8, pred[512,2048]{0,1:T(32,128)(4,1)S(1)} %copy-done.19, s32[512]{0:T(512)S(1)} %copy-done.37, s32[2048]{0:T(1024)S(1)} %copy-done.32), kind=kOutput, calls=%fused_computation.188 | convolution fusion | flops 273677824 | bytes 5910528 | tf_op jit(solution)/shard_map/qd,kd->qk/dot_general | solution.py:89
  103.3 1.5 fusion.64
  104.8 1.7 fusion.78
  106.5 2.1 %fusion.96 = (bf16[32,1,1,64,128]{4,3,2,0,1:T(8,128)(2,1)}, bf16[32,1,1,64,128]{4,3,2,0,1:T(8,128)(2,1)S(1)}) fusion(bf16[32,1,2,64,128]{4,3,2,0,1:T(8,128)(2,1)} %bitcast.227), kind=kLoop, calls=%fused_computation.178 | loop fusion | bytes 2097152 | tf_op jit(solution)/shard_map/slice | solution.py:87
  108.6 3.6 %fusion.104 = (f32[512]{0:T(512)S(1)}, f32[512,2048]{0,1:T(8,128)}) fusion(bf16[2048,128]{1,0:T(8,128)(2,1)S(1)} %bitcast.253, bf16[512,512]{1,0:T(8,128)(2,1)} %param.8, pred[512,2048]{0,1:T(32,128)(4,1)S(1)} %copy-done.18, s32[512]{0:T(512)S(1)} %copy-done.37, s32[2048]{0:T(1024)S(1)} %copy-done.31), kind=kOutput, calls=%fused_computation.186 | convolution fusion | flops 273677824 | bytes 5910528 | tf_op jit(solution)/shard_map/qd,kd->qk/dot_general | solution.py:89
  112.5 2.2 %fusion.76 = f32[8,64,128,1]{2,1,3,0:T(8,128)} fusion(f32[8,64,4,64]{1,3,2,0:T(8,128)S(1)} %get-tuple-element.68, bf16[2,8,4,64,128]{4,3,2,1,0:T(8,128)(2,1)} %bitcast.234, f32[8,64]{1,0:T(8,128)S(1)} %max.47), kind=kOutput, calls=%fused_computation.70 | convolution fusion | flops 33816576 | bytes 1312768 | tf_op jit(solution)/shard_map/wojf,wjfl->wol/dot_general | solution.py:36
  114.7 2.1 %fusion.97 = (bf16[32,1,1,64,128]{4,3,2,0,1:T(8,128)(2,1)}, bf16[32,1,1,64,128]{4,3,2,0,1:T(8,128)(2,1)S(1)}) fusion(bf16[32,1,2,64,128]{4,3,2,0,1:T(8,128)(2,1)} %bitcast.226), kind=kLoop, calls=%fused_computation.179 | loop fusion | bytes 2097152 | tf_op jit(solution)/shard_map/slice | solution.py:87
  116.8 3.7 %fusion.102 = (f32[512]{0:T(512)S(1)}, f32[512,2048]{0,1:T(8,128)}) fusion(bf16[2048,128]{1,0:T(8,128)(2,1)S(1)} %bitcast.254, bf16[512,512]{1,0:T(8,128)(2,1)} %param.8, pred[512,2048]{0,1:T(32,128)(4,1)S(1)} %copy-done.17, s32[512]{0:T(512)S(1)} %copy-done.37, s32[2048]{0:T(1024)S(1)} %copy-done.30), kind=kOutput, calls=%fused_computation.184 | convolution fusion | flops 273677824 | bytes 5910528 | tf_op jit(solution)/shard_map/qd,kd->qk/dot_general | solution.py:89
  120.8 2.2 %fusion.74 = f32[8,64,128,1]{2,1,3,0:T(8,128)} fusion(f32[8,64,4,64]{1,3,2,0:T(8,128)S(1)} %get-tuple-element.64, bf16[2,8,4,64,128]{4,3,2,1,0:T(8,128)(2,1)} %bitcast.232, f32[8,64]{1,0:T(8,128)S(1)} %max.49), kind=kOutput, calls=%fused_computation.69 | convolution fusion | flops 33816576 | bytes 1312768 | tf_op jit(solution)/shard_map/wojf,wjfl->wol/dot_general | solution.py:36
  123.9 3.7 %fusion.100 = (f32[512]{0:T(512)S(1)}, f32[512,2048]{0,1:T(8,128)}) fusion(bf16[2048,128]{1,0:T(8,128)(2,1)S(1)} %bitcast.251, bf16[512,512]{1,0:T(8,128)(2,1)} %param.8, pred[512,2048]{0,1:T(32,128)(4,1)S(1)} %copy-done.16, s32[512]{0:T(512)S(1)} %copy-done.37, s32[2048]{0:T(1024)S(1)} %copy-done.29), kind=kOutput, calls=%fused_computation.182 | convolution fusion | flops 273677824 | bytes 5910528 | tf_op jit(solution)/shard_map/qd,kd->qk/dot_general | solution.py:89
  129.1 3.0 %fusion = f32[512]{0:T(512)S(1)} fusion(f32[512,2048]{0,1:T(8,128)} %get-tuple-element.70, f32[512]{0:T(512)S(1)} %max.44), kind=kLoop, calls=%fused_computation.15 | loop fusion | flops 2096640 | bytes 4198400 | tf_op jit(solution)/shard_map/reduce_sum | solution.py:28
  140.5 35.2 %all-gather.4.cloned.1.call-done = bf16[512,4096]{0,1:T(8,128)(2,1)} async-done(((bf16[512,512]{0,1:T(8,128)(2,1)}), bf16[512,4096]{0,1:T(8,128)(2,1)}) %all-gather.4.cloned.1.call-update) | async-done | bytes 4194320 | tf_op jit(solution)/shard_map/all_gather | solution.py:131
  175.7 6.6 %convolution_convert_fusion = bf16[512,512]{1,0:T(8,128)(2,1)} fusion(bf16[512,4096]{0,1:T(8,128)(2,1)} %all-gather.4.cloned.1.call-done, bf16[4096,512]{1,0:T(8,128)(2,1)} %param.15), kind=kOutput, calls=%fused_computation.43 | convolution fusion | flops 2147745792 | bytes 8912896 | tf_op jit(solution)/shard_map/dot_general | solution.py:130
  (210 shorter events, 37.8 us)
Async XLA Ops:
  6.5 13.9 %copy-start.28 = (s32[4,32,1]{1,2,0:T(1,128)S(1)}, s32[4,32,1]{1,2,0:T(1,128)}, u32[]{:S(2)}) copy-start(s32[4,32,1]{1,2,0:T(1,128)} %param.13) | copy-start | bytes 1540
  6.5 13.4 %copy-start.35 = (s32[4,4]{1,0:T(4,128)S(1)}, s32[4,4]{1,0:T(4,128)}, u32[]{:S(2)}) copy-start(s32[4,4]{1,0:T(4,128)} %param.11) | copy-start | bytes 196
  6.5 14.2 %copy-start.36 = (s32[4,32]{1,0:T(4,128)S(1)}, s32[4,32]{1,0:T(4,128)}, u32[]{:S(2)}) copy-start(s32[4,32]{1,0:T(4,128)} %param.14) | copy-start | bytes 1540
  6.5 87.8 %all-gather.6.cloned.1.call-start = ((), (), s32[]{:S(2)}) async-start(), calls=%async_computation.1 | async-start | bytes 4325376 | tf_op jit(solution)/shard_map/all_gather | solution.py:68
  11.3 164.4 %all-gather.4.cloned.1.call-start = ((), (), s32[]{:S(2)}) async-start(), calls=%async_computation | async-start | bytes 4718592 | tf_op jit(solution)/shard_map/all_gather | solution.py:131
  12.4 35.8 %collective-permute-start = (bf16[2,512,128]{2,1,0:T(8,128)(2,1)S(1)}, bf16[2,512,128]{2,1,0:T(8,128)(2,1)S(1)}, u32[]{:S(2)}, u32[]{:S(2)}) collective-permute-start(bf16[2,512,128]{2,1,0:T(8,128)(2,1)S(1)} %pad_maximum_fusion.2), channel_id=1, source_target_pairs={{0,8},{8,16},{16,24},{24,32},{32,40},{40,48},{48,56},{56,64},{64,7... | collective-permute-start | bytes 786440 | tf_op jit(solution)/shard_map/ppermute | solution.py:15
  35.9 11.5 %copy-start.22 = (bf16[512,512]{1,0:T(8,128)(2,1)S(1)}, bf16[512,512]{1,0:T(8,128)(2,1)}, u32[]{:S(2)}) copy-start(bf16[512,512]{1,0:T(8,128)(2,1)} %param.8) | copy-start | bytes 1572868
  35.9 12.2 %copy-start.14 = (bf16[512,128]{1,0:T(8,128)(2,1)S(1)}, bf16[512,128]{1,0:T(8,128)(2,1)}, u32[]{:S(2)}) copy-start(bf16[512,128]{1,0:T(8,128)(2,1)} %param.10) | copy-start | bytes 393220
  35.9 12.2 %copy-start.15 = (bf16[512,128]{1,0:T(8,128)(2,1)S(1)}, bf16[512,128]{1,0:T(8,128)(2,1)}, u32[]{:S(2)}) copy-start(bf16[512,128]{1,0:T(8,128)(2,1)} %param.9) | copy-start | bytes 393220
  55.1 6.1 %copy-start.24 = (pred[64,4,64]{0,2,1:T(8,128)(4,1)S(1)}, pred[64,4,64]{0,2,1:T(8,128)(4,1)}, u32[]{:S(2)}) copy-start(pred[64,4,64]{0,2,1:T(8,128)(4,1)} %get-tuple-element.24) | copy-start | bytes 49156
  55.1 6.1 %copy-start.38 = (pred[8,4]{1,0:T(8,128)(4,1)S(1)}, pred[8,4]{1,0:T(8,128)(4,1)}, u32[]{:S(2)}) copy-start(pred[8,4]{1,0:T(8,128)(4,1)} %get-tuple-element.52) | copy-start | bytes 100
  61.6 38.0 %copy-start.32 = (s32[2048]{0:T(1024)S(1)}, s32[2048]{0:T(1024)}, u32[]{:S(2)}) copy-start(s32[2048]{0:T(1024)} %add.293) | copy-start | bytes 24580
  61.6 38.0 %copy-start.37 = (s32[512]{0:T(512)S(1)}, s32[512]{0:T(512)}, u32[]{:S(2)}) copy-start(s32[512]{0:T(512)} %iota_add_fusion.4) | copy-start | bytes 6148
  94.4 5.3 %copy-start.19 = (pred[512,2048]{0,1:T(32,128)(4,1)S(1)}, pred[512,2048]{0,1:T(32,128)(4,1)}, u32[]{:S(2)}) copy-start(pred[512,2048]{0,1:T(32,128)(4,1)} %reshape.1051) | copy-start | bytes 3145732
  99.6 8.9 %copy-start.31 = (s32[2048]{0:T(1024)S(1)}, s32[2048]{0:T(1024)}, u32[]{:S(2)}) copy-start(s32[2048]{0:T(1024)} %add.307) | copy-start | bytes 24580
  103.3 5.3 %copy-start.18 = (pred[512,2048]{0,1:T(32,128)(4,1)S(1)}, pred[512,2048]{0,1:T(32,128)(4,1)}, u32[]{:S(2)}) copy-start(pred[512,2048]{0,1:T(32,128)(4,1)} %reshape.1054) | copy-start | bytes 3145732
  108.6 8.2 %copy-start.30 = (s32[2048]{0:T(1024)S(1)}, s32[2048]{0:T(1024)}, u32[]{:S(2)}) copy-start(s32[2048]{0:T(1024)} %add.314) | copy-start | bytes 24580
  116.8 6.2 %copy-start.4 = (bf16[1,64,64,128]{3,2,1,0:T(8,128)(2,1)S(1)}, bf16[1,64,64,128]{3,2,1,0:T(8,128)(2,1)}, u32[]{:S(2)}) copy-start(bf16[1,64,64,128]{3,2,1,0:T(8,128)(2,1)} %get-tuple-element.8) | copy-start | bytes 3145732
  116.8 7.0 %copy-start.29 = (s32[2048]{0:T(1024)S(1)}, s32[2048]{0:T(1024)}, u32[]{:S(2)}) copy-start(s32[2048]{0:T(1024)} %add.321) | copy-start | bytes 24580
  123.8 4.7 %copy-start.20 = (f32[8,64,128,1]{2,1,3,0:T(8,128)S(1)}, f32[8,64,128,1]{2,1,3,0:T(8,128)}, u32[]{:S(2)}) copy-start(f32[8,64,128,1]{2,1,3,0:T(8,128)} %fusion.76) | copy-start | bytes 786436
  123.8 4.8 %copy-start.34 = (f32[512]{0:T(512)S(1)}, f32[512]{0:T(512)}, u32[]{:S(2)}) copy-start(f32[512]{0:T(512)} %reduce_max.98) | copy-start | bytes 6148
  123.9 4.9 %copy-start.21 = (f32[8,64,128,1]{2,1,3,0:T(8,128)S(1)}, f32[8,64,128,1]{2,1,3,0:T(8,128)}, u32[]{:S(2)}) copy-start(f32[8,64,128,1]{2,1,3,0:T(8,128)} %fusion.74) | copy-start | bytes 786436
  128.9 6.9 %copy-start.10 = (bf16[32,1,1,64,128]{4,3,2,0,1:T(8,128)(2,1)S(1)}, bf16[32,1,1,64,128]{4,3,2,0,1:T(8,128)(2,1)}, u32[]{:S(2)}) copy-start(bf16[32,1,1,64,128]{4,3,2,0,1:T(8,128)(2,1)} %get-tuple-element.9) | copy-start | bytes 1572868
  129.1 4.7 %copy-start.2 = (f32[512,2048]{0,1:T(8,128)S(1)}, f32[512,2048]{0,1:T(8,128)}, u32[]{:S(2)}) copy-start(f32[512,2048]{0,1:T(8,128)} %get-tuple-element.62) | copy-start | bytes 12582916
  (21 other events, 61.5 us)
Sparse Core Ops, SparseCore 0:
  11.4 82.9 all-gather.5
  140.6 35.0 all-gather.3
where the time goes:
time: 190 us; the launch traced here: 189 us
  waiting for transfers between devices  68 us (36%)
  local copies, waits for them, and re-layouts  56.4 us (30%)
  matrix products  33.1 us (17%)
  between operations  14.1 us (7%)
  other arithmetic  13.2 us (7%)
  starting transfers between devices  4.43 us (2%)
    all_gather x1, waiting for transfers between devices, shards(): lax.all_gather(attended, 'head', axis=1, tiled=True)  35.2 us
    all_gather x1, waiting for transfers between devices, shards(): gathered = lax.all_gather(block_rows[:, None], 'ctx', axis=1, tiled=True)  32.7 us
    reshape x4, local copies, waits for them, and re-layouts, shards(): vert_mask = jnp.broadcast_to(block_mask[:, None, :, None], (per_dev, BLOC...  18.9 us
    dot_general x4, matrix products, shards(): jnp.einsum('qd,kd->qk', query_head, vert_keys, preferred_element_type=jnp...  14.6 us
    unnamed x88, local copies, waits for them, and re-layouts  6.68 us
    dot_general x1, matrix products, shards(): jnp.dot(lax.all_gather(attended, 'head', axis=1, tiled=True), out_weight,...  6.61 us
    dot_general x4, matrix products, attend(): jnp.einsum('wojf,wjfl->wol', slash_probability, diagonal_values, preferre...  6.35 us
    slice x4, local copies, waits for them, and re-layouts, shards(): vertical[:, :, 1].reshape(slot_count * BLOCK_TOKENS, HEAD_SIZE)  5.9 us
  transfers between devices with their start and end apart: 3, of which 2 were waited for; matrix products, arithmetic and copies ran while one was open for 22% of the time, Pallas kernels for 0%

commit v1 on v0

--- a/solution.py
+++ b/solution.py
@@ -65,7 +65,9 @@
     mine_picks = lax.dynamic_index_in_dim(head_picks, device_rank, 1, keepdims=False)
     chosen_local = jnp.take_along_axis(mine_union[head_group], mine_picks, axis=1)
     block_rows = local_blocks[:, chosen_local, :, head_group[:, None], :]
-    gathered = lax.all_gather(block_rows[:, None], "ctx", axis=1, tiled=True)
+    gathered = jnp.concatenate(
+        lax.all_to_all(jnp.stack([block_rows[:, None]] * lax.axis_size("ctx")), "ctx", 0, 0), axis=1
+    )
     slot_block = owner_base[None] + jnp.take_along_axis(
         union_blocks[head_group], head_picks, axis=2
     )

time: 190 us -> 234 us (1.23)
  waiting for transfers between devices: 68 us -> 101 us
  starting transfers between devices: 4.43 us -> 15.3 us
    ppermute x1, waiting for transfers between devices: 0.01 us -> 62.5 us  [from_behind(): return lax.ppermute(array, axis, pairs)]
    all_gather x1 -> x0, waiting for transfers between devices: 32.7 us -> none  [shards(): gathered = lax.all_gather(block_rows[:, None], 'ctx', axis=1, tiled=True)]
    all_to_all x0 -> x1, starting transfers between devices: none -> 12.1 us  [shards(): lax.all_to_all(jnp.stack([block_rows[:, None]] * lax.axis_size('ctx')), '...]
    squeeze x0 -> x1, local copies, waits for them, and re-layouts: none -> 5.04 us  [shards(): vertical = gathered[source_of[head_index]]]
    slice x1 -> x0, local copies, waits for them, and re-layouts: 4.36 us -> none  [shards(): vertical = gathered[source_of[head_index]]]
    all_gather x1, waiting for transfers between devices: 35.2 us -> 38.6 us  [shards(): lax.all_gather(attended, 'head', axis=1, tiled=True)]
    another operation x0 -> x1, local copies, waits for them, and re-layouts: none -> 3.03 us  [shards(): jnp.stack([block_rows[:, None]] * lax.axis_size('ctx'))]
    unnamed x88 -> x90, local copies, waits for them, and re-layouts: 6.68 us -> 6.67 us
  transfers between devices with their start and end apart: 3 -> 3, of which waited for: 2 -> 2; matrix products, arithmetic and copies ran while one was open for 22% -> 17% of each run, Pallas kernels for 0% -> 0%
where the time goes in v1:
time: 234 us
  waiting for transfers between devices  101 us (43%)
  local copies, waits for them, and re-layouts  58.7 us (25%)
  matrix products  33 us (14%)
  starting transfers between devices  15.3 us (7%)
  between operations  14.2 us (6%)
  other arithmetic  11.5 us (5%)
    ppermute x1, waiting for transfers between devices, from_behind(): return lax.ppermute(array, axis, pairs)  62.5 us
    all_gather x1, waiting for transfers between devices, shards(): lax.all_gather(attended, 'head', axis=1, tiled=True)  38.6 us
    reshape x4, local copies, waits for them, and re-layouts, shards(): vert_mask = jnp.broadcast_to(block_mask[:, None, :, None], (per_dev, BLOC...  18.9 us
    dot_general x4, matrix products, shards(): jnp.einsum('qd,kd->qk', query_head, vert_keys, preferred_element_type=jnp...  14.6 us
    all_to_all x1, starting transfers between devices, shards(): lax.all_to_all(jnp.stack([block_rows[:, None]] * lax.axis_size('ctx')), '...  12.1 us
    unnamed x90, local copies, waits for them, and re-layouts  6.67 us
    dot_general x1, matrix products, shards(): jnp.dot(lax.all_gather(attended, 'head', axis=1, tiled=True), out_weight,...  6.61 us
    dot_general x4, matrix products, attend(): jnp.einsum('wojf,wjfl->wol', slash_probability, diagonal_values, preferre...  6.35 us
  transfers between devices with their start and end apart: 3, of which 2 were waited for; matrix products, arithmetic and copies ran while one was open for 17% of the time, Pallas kernels for 0%

profile of v1, /device:TPU:1, one launch (start us, length us, event | category | flops | bytes accessed | tf_op | source)
XLA Modules:
  0.0 233.8 jit_solution(8045088279705437814)
XLA Ops:
  10.6 3.0 %stack.21 = bf16[32,4,1,1,2,64,128]{6,5,4,3,2,1,0:T(8,128)(2,1)} broadcast(bf16[4,2,64,128]{3,2,1,0:T(8,128)(2,1)S(1)} %gather_fusion), dimensions={1,4,5,6} | broadcast | bytes 4325376 | tf_op jit(solution)/shard_map/stack | solution.py:69
  13.6 12.1 %all-to-all-start = ((bf16[32,4,1,1,2,64,128]{6,5,4,3,2,1,0:T(8,128)(2,1)}), bf16[32,4,1,1,2,64,128]{6,5,4,3,2,1,0:T(8,128)(2,1)}, u32[]{:S(2)}, u32[]{:S(2)}) async-start(bf16[32,4,1,1,2,64,128]{6,5,4,3,2,1,0:T(8,128)(2,1)} %stack.21), calls=%async_computation | async-start | bytes 8388608 | tf_op jit(solution)/shard_map/all_to_all | solution.py:69
  25.9 3.1 %collective-permute-start = (bf16[2,512,128]{2,1,0:T(8,128)(2,1)S(1)}, bf16[2,512,128]{2,1,0:T(8,128)(2,1)S(1)}, u32[]{:S(2)}, u32[]{:S(2)}) collective-permute-start(bf16[2,512,128]{2,1,0:T(8,128)(2,1)S(1)} %pad_maximum_fusion.2), channel_id=1, source_target_pairs={{0,8},{8,16},{16,24},{24,32},{32,40},{40,48},{48,56},{56,64},{64,7... | collective-permute-start | bytes 786440 | tf_op jit(solution)/shard_map/ppermute | solution.py:15
  29.2 1.5 gather_fusion.5
  34.5 4.7 %reshape.1066 = pred[512,2048]{0,1:T(32,128)(4,1)} reshape(pred[8,64,32,64]{1,0,3,2:T(8,128)(4,1)S(1)} %broadcast_in_dim.26) | data formatting | bytes 2097152 | tf_op jit(solution)/shard_map/reshape | solution.py:100
  40.6 4.7 %reshape.1070 = pred[512,2048]{0,1:T(32,128)(4,1)} reshape(pred[8,64,32,64]{1,0,3,2:T(8,128)(4,1)S(1)} %broadcast_in_dim.30) | data formatting | bytes 2097152 | tf_op jit(solution)/shard_map/reshape | solution.py:100
  46.8 4.7 %reshape.1073 = pred[512,2048]{0,1:T(32,128)(4,1)} reshape(pred[8,64,32,64]{1,0,3,2:T(8,128)(4,1)S(1)} %broadcast_in_dim.31) | data formatting | bytes 2097152 | tf_op jit(solution)/shard_map/reshape | solution.py:100
  52.8 4.7 %reshape.1076 = pred[512,2048]{0,1:T(32,128)(4,1)} reshape(pred[8,64,32,64]{1,0,3,2:T(8,128)(4,1)S(1)} %broadcast_in_dim.32) | data formatting | bytes 2097152 | tf_op jit(solution)/shard_map/reshape | solution.py:100
  59.0 62.5 %collective-permute-done = bf16[2,512,128]{2,1,0:T(8,128)(2,1)S(1)} collective-permute-done((bf16[2,512,128]{2,1,0:T(8,128)(2,1)S(1)}, bf16[2,512,128]{2,1,0:T(8,128)(2,1)S(1)}, u32[]{:S(2)}, u32[]{:S(2)}) %collective-permute-start) | collective-permute-done | bytes 262176 | tf_op jit(solution)/shard_map/ppermute | solution.py:15
  130.6 1.7 gather_fusion.4
  135.0 5.0 %slice_bitcast_fusion.3 = (bf16[32,1,2,64,128]{4,3,2,0,1:T(8,128)(2,1)S(1)}, bf16[32,1,2,64,128]{4,3,2,0,1:T(8,128)(2,1)}, bf16[32,1,2,64,128]{4,3,2,0,1:T(8,128)(2,1)}, bf16[32,1,2,64,128]{4,3,2,0,1:T(8,128)(2,1)}) fusion(bf16[4,32,1,1,2,64,128]{6,5,4,3,2,0,1:T(8,128)(2,1)} %bitcast.16), kind=kLoop, calls=%fused_computation.59 | loop fusion | bytes 8388608 | tf_op jit(solution)/shard_map/squeeze | solution.py:84
  140.9 3.6 %fusion.105 = (f32[512]{0:T(512)S(1)}, f32[512,2048]{0,1:T(8,128)}) fusion(bf16[2048,128]{1,0:T(8,128)(2,1)S(1)} %bitcast.253, bf16[512,512]{1,0:T(8,128)(2,1)} %param.8, pred[512,2048]{0,1:T(32,128)(4,1)S(1)} %copy-done.19, s32[512]{0:T(512)S(1)} %copy-done.38, s32[2048]{0:T(1024)S(1)} %copy-done.32), kind=kOutput, calls=%fused_computation.191 | convolution fusion | flops 273677824 | bytes 5910528 | tf_op jit(solution)/shard_map/qd,kd->qk/dot_general | solution.py:91
  144.6 1.5 fusion.64
  146.1 1.7 fusion.78
  147.8 2.1 fusion.95
  149.9 3.6 %fusion.103 = (f32[512]{0:T(512)S(1)}, f32[512,2048]{0,1:T(8,128)}) fusion(bf16[2048,128]{1,0:T(8,128)(2,1)S(1)} %bitcast.254, bf16[512,512]{1,0:T(8,128)(2,1)} %param.8, pred[512,2048]{0,1:T(32,128)(4,1)S(1)} %copy-done.18, s32[512]{0:T(512)S(1)} %copy-done.38, s32[2048]{0:T(1024)S(1)} %copy-done.31), kind=kOutput, calls=%fused_computation.189 | convolution fusion | flops 273677824 | bytes 5910528 | tf_op jit(solution)/shard_map/qd,kd->qk/dot_general | solution.py:91
  153.8 2.2 fusion.76
  156.0 2.1 fusion.96
  158.1 3.7 %fusion.101 = (f32[512]{0:T(512)S(1)}, f32[512,2048]{0,1:T(8,128)}) fusion(bf16[2048,128]{1,0:T(8,128)(2,1)S(1)} %bitcast.255, bf16[512,512]{1,0:T(8,128)(2,1)} %param.8, pred[512,2048]{0,1:T(32,128)(4,1)S(1)} %copy-done.17, s32[512]{0:T(512)S(1)} %copy-done.38, s32[2048]{0:T(1024)S(1)} %copy-done.30), kind=kOutput, calls=%fused_computation.187 | convolution fusion | flops 273677824 | bytes 5910528 | tf_op jit(solution)/shard_map/qd,kd->qk/dot_general | solution.py:91
  162.1 2.2 fusion.74
  165.2 3.7 %fusion.99 = (f32[512]{0:T(512)S(1)}, f32[512,2048]{0,1:T(8,128)}) fusion(bf16[2048,128]{1,0:T(8,128)(2,1)S(1)} %bitcast.252, bf16[512,512]{1,0:T(8,128)(2,1)} %param.8, pred[512,2048]{0,1:T(32,128)(4,1)S(1)} %copy-done.16, s32[512]{0:T(512)S(1)} %copy-done.38, s32[2048]{0:T(1024)S(1)} %copy-done.29), kind=kOutput, calls=%fused_computation.185 | convolution fusion | flops 273677824 | bytes 5910528 | tf_op jit(solution)/shard_map/qd,kd->qk/dot_general | solution.py:91
  170.4 3.0 %fusion = f32[512]{0:T(512)S(1)} fusion(f32[512,2048]{0,1:T(8,128)} %get-tuple-element.70, f32[512]{0:T(512)S(1)} %max.44), kind=kLoop, calls=%fused_computation.15 | loop fusion | flops 2096640 | bytes 4198400 | tf_op jit(solution)/shard_map/reduce_sum | solution.py:28
  181.8 38.6 %all-gather.2.cloned.1.call-done = bf16[512,4096]{0,1:T(8,128)(2,1)} async-done(((bf16[512,512]{0,1:T(8,128)(2,1)}), bf16[512,4096]{0,1:T(8,128)(2,1)}) %all-gather.2.cloned.1.call-update) | async-done | bytes 4194320 | tf_op jit(solution)/shard_map/all_gather | solution.py:133
  220.3 6.6 %convolution_convert_fusion = bf16[512,512]{1,0:T(8,128)(2,1)} fusion(bf16[512,4096]{0,1:T(8,128)(2,1)} %all-gather.2.cloned.1.call-done, bf16[4096,512]{1,0:T(8,128)(2,1)} %param.15), kind=kOutput, calls=%fused_computation.43 | convolution fusion | flops 2147745792 | bytes 8912896 | tf_op jit(solution)/shard_map/dot_general | solution.py:132
  (212 shorter events, 37.3 us)
Async XLA Ops:
  13.6 12.2 %copy-start.14 = (bf16[512,128]{1,0:T(8,128)(2,1)S(1)}, bf16[512,128]{1,0:T(8,128)(2,1)}, u32[]{:S(2)}) copy-start(bf16[512,128]{1,0:T(8,128)(2,1)} %param.10) | copy-start | bytes 393220
  13.6 12.2 %copy-start.15 = (bf16[512,128]{1,0:T(8,128)(2,1)S(1)}, bf16[512,128]{1,0:T(8,128)(2,1)}, u32[]{:S(2)}) copy-start(bf16[512,128]{1,0:T(8,128)(2,1)} %param.9) | copy-start | bytes 393220
  13.6 15.4 %copy-start.28 = (s32[4,32,1]{1,2,0:T(1,128)S(1)}, s32[4,32,1]{1,2,0:T(1,128)}, u32[]{:S(2)}) copy-start(s32[4,32,1]{1,2,0:T(1,128)} %param.13) | copy-start | bytes 1540
  13.6 15.5 %copy-start.36 = (s32[1,32,2]{1,2,0:T(2,128)S(1)}, s32[1,32,2]{1,2,0:T(2,128)}, u32[]{:S(2)}) copy-start(s32[1,32,2]{1,2,0:T(2,128)} %param.12) | copy-start | bytes 772
  13.6 17.2 %copy-start.35 = (s32[4,4]{1,0:T(4,128)S(1)}, s32[4,4]{1,0:T(4,128)}, u32[]{:S(2)}) copy-start(s32[4,4]{1,0:T(4,128)} %param.11) | copy-start | bytes 196
  13.6 18.0 %copy-start.37 = (s32[4,32]{1,0:T(4,128)S(1)}, s32[4,32]{1,0:T(4,128)}, u32[]{:S(2)}) copy-start(s32[4,32]{1,0:T(4,128)} %param.14) | copy-start | bytes 1540
  13.6 121.4 %all-to-all-start = ((bf16[32,4,1,1,2,64,128]{6,5,4,3,2,1,0:T(8,128)(2,1)}), bf16[32,4,1,1,2,64,128]{6,5,4,3,2,1,0:T(8,128)(2,1)}, u32[]{:S(2)}, u32[]{:S(2)}) async-start(bf16[32,4,1,1,2,64,128]{6,5,4,3,2,1,0:T(8,128)(2,1)} %stack.21), calls=%async_computation | async-start | bytes 8388608 | tf_op jit(solution)/shard_map/all_to_all | solution.py:69
  25.8 194.6 %all-gather.2.cloned.1.call-start = ((), (), s32[]{:S(2)}) async-start(), calls=%async_computation.1 | async-start | bytes 4718592 | tf_op jit(solution)/shard_map/all_gather | solution.py:133
  25.9 95.6 %collective-permute-start = (bf16[2,512,128]{2,1,0:T(8,128)(2,1)S(1)}, bf16[2,512,128]{2,1,0:T(8,128)(2,1)S(1)}, u32[]{:S(2)}, u32[]{:S(2)}) collective-permute-start(bf16[2,512,128]{2,1,0:T(8,128)(2,1)S(1)} %pad_maximum_fusion.2), channel_id=1, source_target_pairs={{0,8},{8,16},{16,24},{24,32},{32,40},{40,48},{48,56},{56,64},{64,7... | collective-permute-start | bytes 786440 | tf_op jit(solution)/shard_map/ppermute | solution.py:15
  46.7 11.5 %copy-start.22 = (bf16[512,512]{1,0:T(8,128)(2,1)S(1)}, bf16[512,512]{1,0:T(8,128)(2,1)}, u32[]{:S(2)}) copy-start(bf16[512,512]{1,0:T(8,128)(2,1)} %param.8) | copy-start | bytes 1572868
  57.5 65.8 %copy-start.27 = (pred[64,4,64]{0,2,1:T(8,128)(4,1)S(1)}, pred[64,4,64]{0,2,1:T(8,128)(4,1)}, u32[]{:S(2)}) copy-start(pred[64,4,64]{0,2,1:T(8,128)(4,1)} %get-tuple-element.21) | copy-start | bytes 49156
  57.5 65.8 %copy-start.42 = (pred[8,4]{1,0:T(8,128)(4,1)S(1)}, pred[8,4]{1,0:T(8,128)(4,1)}, u32[]{:S(2)}) copy-start(pred[8,4]{1,0:T(8,128)(4,1)} %get-tuple-element.49) | copy-start | bytes 100
  128.4 6.1 %copy-start.24 = (pred[64,4,64]{0,2,1:T(8,128)(4,1)S(1)}, pred[64,4,64]{0,2,1:T(8,128)(4,1)}, u32[]{:S(2)}) copy-start(pred[64,4,64]{0,2,1:T(8,128)(4,1)} %get-tuple-element.24) | copy-start | bytes 49156
  128.5 6.1 %copy-start.39 = (pred[8,4]{1,0:T(8,128)(4,1)S(1)}, pred[8,4]{1,0:T(8,128)(4,1)}, u32[]{:S(2)}) copy-start(pred[8,4]{1,0:T(8,128)(4,1)} %get-tuple-element.52) | copy-start | bytes 100
  135.0 5.9 %copy-start.19 = (pred[512,2048]{0,1:T(32,128)(4,1)S(1)}, pred[512,2048]{0,1:T(32,128)(4,1)}, u32[]{:S(2)}) copy-start(pred[512,2048]{0,1:T(32,128)(4,1)} %reshape.1066) | copy-start | bytes 3145732
  135.0 5.9 %copy-start.32 = (s32[2048]{0:T(1024)S(1)}, s32[2048]{0:T(1024)}, u32[]{:S(2)}) copy-start(s32[2048]{0:T(1024)} %add.293) | copy-start | bytes 24580
  135.0 5.9 %copy-start.38 = (s32[512]{0:T(512)S(1)}, s32[512]{0:T(512)}, u32[]{:S(2)}) copy-start(s32[512]{0:T(512)} %iota_add_fusion.4) | copy-start | bytes 6148
  140.9 8.9 %copy-start.31 = (s32[2048]{0:T(1024)S(1)}, s32[2048]{0:T(1024)}, u32[]{:S(2)}) copy-start(s32[2048]{0:T(1024)} %add.307) | copy-start | bytes 24580
  144.6 5.3 %copy-start.18 = (pred[512,2048]{0,1:T(32,128)(4,1)S(1)}, pred[512,2048]{0,1:T(32,128)(4,1)}, u32[]{:S(2)}) copy-start(pred[512,2048]{0,1:T(32,128)(4,1)} %reshape.1070) | copy-start | bytes 3145732
  149.9 8.2 %copy-start.30 = (s32[2048]{0:T(1024)S(1)}, s32[2048]{0:T(1024)}, u32[]{:S(2)}) copy-start(s32[2048]{0:T(1024)} %add.314) | copy-start | bytes 24580
  158.1 6.2 %copy-start.4 = (bf16[32,1,2,64,128]{4,3,2,0,1:T(8,128)(2,1)S(1)}, bf16[32,1,2,64,128]{4,3,2,0,1:T(8,128)(2,1)}, u32[]{:S(2)}) copy-start(bf16[32,1,2,64,128]{4,3,2,0,1:T(8,128)(2,1)} %get-tuple-element.6) | copy-start | bytes 3145732
  158.1 7.0 %copy-start.29 = (s32[2048]{0:T(1024)S(1)}, s32[2048]{0:T(1024)}, u32[]{:S(2)}) copy-start(s32[2048]{0:T(1024)} %add.321) | copy-start | bytes 24580
  165.2 4.9 %copy-start.21 = (f32[8,64,128,1]{2,1,3,0:T(8,128)S(1)}, f32[8,64,128,1]{2,1,3,0:T(8,128)}, u32[]{:S(2)}) copy-start(f32[8,64,128,1]{2,1,3,0:T(8,128)} %fusion.74) | copy-start | bytes 786436
  170.2 6.9 %copy-start.10 = (bf16[32,1,1,64,128]{4,3,2,0,1:T(8,128)(2,1)S(1)}, bf16[32,1,1,64,128]{4,3,2,0,1:T(8,128)(2,1)}, u32[]{:S(2)}) copy-start(bf16[32,1,1,64,128]{4,3,2,0,1:T(8,128)(2,1)} %get-tuple-element.9) | copy-start | bytes 1572868
  (22 other events, 69.0 us)
Sparse Core Ops, SparseCore 0:
  181.9 38.4 all-gather.1
